TPU v7x, 256 devices: a whole 4x4x8 slice. The times are simulated.
256 devices in a mesh: prow: 16 (over y, x), pcol: 16 (over z, core).
Axes of the slice: x: 4, y: 4, z: 8, core: 2. Of those that a mesh axis runs over, the one named last changes fastest.
Arguments:
- matrix: float32 [5, 16, 256, 5, 16, 256], P(None, 'prow', None, None, 'pcol')
Outputs:
- factored: float32 [5, 16, 256, 5, 16, 256], P(None, 'prow', None, None, 'pcol')
All inputs are finite; a program needn't handle non-finite values.
Results may differ from a plain program's by a relative error of at most 0.0003.
Values sent between devices are 32-bit elements; how exact they have to be, the bound alone decides.
A program may use at most 128 MiB of HBM per device.

v0:
```python
import jax
import jax.numpy as jnp
from jax import lax
from jax.sharding import PartitionSpec as P


def broadcast(value, axis, source):
    kept = jnp.where(lax.axis_index(axis) == source, value, 0).astype(value.dtype)
    return lax.psum(kept, axis)


def panel_solve(factor, tiles, grid_row):
    count, width = (tiles.shape[0], tiles.shape[1])
    solved = lax.linalg.triangular_solve(
        factor, tiles.reshape(count * width, width), left_side=False, lower=True, transpose_a=True
    )
    solved = solved.reshape(count, width, width)
    return solved.at[0].set(jnp.where(grid_row == 0, factor, solved[0]))


def per_device(matrix):
    grid_row = lax.axis_index("prow")
    grid_col = lax.axis_index("pcol")
    n_row = lax.axis_size("prow")
    n_col = lax.axis_size("pcol")
    local = matrix[:, 0, :, :, 0, :]
    tile_rows, width, tile_cols = (local.shape[0], local.shape[1], local.shape[2])
    column = local[:, :, 0, :]
    leading = broadcast(local[0, :, 0, :], "prow", 0)
    factor = jnp.linalg.cholesky(leading)
    solved = panel_solve(factor, column, grid_row)
    row_tiles = broadcast(solved, "pcol", 0)
    every = lax.all_gather(row_tiles[:, None], "prow", axis=1, tiled=True)
    col_tiles = lax.dynamic_index_in_dim(every, grid_col, 1, keepdims=False)
    product = jnp.einsum("kab,cdb->kacd", row_tiles, col_tiles, precision=lax.Precision.HIGHEST)
    updated = local - product
    row_global = jnp.arange(tile_rows, dtype=jnp.int32) * n_row + grid_row
    col_global = jnp.arange(tile_cols, dtype=jnp.int32) * n_col + grid_col
    lower = (row_global[:, None] >= col_global[None, :])[:, None, :, None]
    result = jnp.where(lower, updated, jnp.zeros_like(updated))
    first = (col_global == 0)[None, None, :, None]
    result = jnp.where(first, row_tiles[:, :, None, :], result)
    return result[:, None, :, :, None, :]


def solution(mesh):
    return jax.shard_map(
        per_device,
        mesh=mesh,
        in_specs=(P(None, "prow", None, None, "pcol", None),),
        out_specs=P(None, "prow", None, None, "pcol", None),
        check_vma=False,
    )
```

profile of v0, /device:TPU:1, one launch (start us, length us, event | category | flops | bytes accessed | tf_op | source)
XLA Modules:
  0.0 470.3 jit_solution(5706989088490152155)
XLA Ops:
  6.5 0.0 all-reduce.4.cloned.1.call-start
  6.5 14.1 %copy.10 = f32[5,1,256,5,1,256]{2,5,3,0,4,1:T(8,128)} copy(f32[5,1,256,5,1,256]{5,4,3,2,1,0:T(1,128)} %param.3) | data formatting | bytes 13107200 | tf_op args[0]
  20.7 1.7 fusion.9
  22.3 0.0 all-reduce.4.cloned.1.call-update
  22.4 0.0 all-reduce.6.cloned.1.call-start
  22.4 1.4 slice.87
  23.8 0.4 copy.12
  24.3 95.1 %all-reduce.4.cloned.1.call-done = f32[256,256]{0,1:T(8,128)} async-done(((f32[256,256]{0,1:T(8,128)}), f32[256,256]{0,1:T(8,128)}) %all-reduce.4.cloned.1.call-update) | async-done | bytes 262160 | tf_op jit(solution)/shard_map/psum | solution.py:9
  119.4 1.1 copy.11
  120.5 1.0 fusion.10
  121.5 11.7 %cholesky.49 = f32[128,128]{1,0:T(8,128)S(1)} custom-call(f32[128,128]{1,0:T(8,128)S(1)} %cholesky.115), custom_call_target="Cholesky" | custom-call | tf_op jit(solution)/shard_map/jit(cholesky)/cholesky | solution.py:30
  133.2 9.8 %custom-call.14 = f32[1,128,128]{1,2,0:T(8,128)S(1)} custom-call(f32[1,128,128]{2,1,0:T(8,128)S(1)} %get-tuple-element.38), custom_call_target="InvertDiagBlocksLowerTriangular" | custom-call | tf_op jit(solution)/shard_map/jit(cholesky)/cholesky | solution.py:30
  143.1 0.2 constant_dynamic-update-slice_fusion
  143.3 0.3 convolution_subtract_fusion.1
  143.5 11.7 %cholesky.103 = f32[128,128]{1,0:T(8,128)S(1)} custom-call(f32[128,128]{1,0:T(8,128)S(1)} %convolution_subtract_fusion.1), custom_call_target="Cholesky" | custom-call | tf_op jit(solution)/shard_map/jit(cholesky)/cholesky | solution.py:30
  155.3 0.7 compare_reduce_fusion
  157.3 0.1 triangular_solve.59
  157.4 4.2 while.2
  157.5 0.7 fusion.26
  158.2 1.3 bitcast_dynamic-update-slice_fusion.2
  159.6 0.7 fusion.26
  160.2 1.3 bitcast_dynamic-update-slice_fusion.2
  161.6 19.7 %custom-call.15 = f32[2,128,128]{1,2,0:T(8,128)S(1)} custom-call(f32[2,128,128]{2,1,0:T(8,128)S(1)} %get-tuple-element.24), custom_call_target="InvertDiagBlocksLowerTriangular" | custom-call | tf_op jit(solution)/shard_map/triangular_solve | solution.py:14
  181.3 0.8 fusion.3
  182.0 1.2 convolution_subtract_fusion
  183.2 0.2 copy.13
  183.5 0.7 fusion.12
  184.1 0.1 pad_maximum_fusion
  184.3 1.2 broadcast_select_fusion
  185.5 0.0 all-reduce.6.cloned.1.call-update
  185.5 0.0 all-gather.3.cloned.1.call-start
  185.5 113.2 %all-reduce.6.cloned.1.call-done = f32[5,256,256]{2,1,0:T(8,128)} async-done(((f32[5,256,256]{2,1,0:T(8,128)}), f32[5,256,256]{2,1,0:T(8,128)}) %all-reduce.6.cloned.1.call-update) | async-done | bytes 1310736 | tf_op jit(solution)/shard_map/psum | solution.py:9
  298.7 0.0 copy-start
  298.7 0.0 all-gather.3.cloned.1.call-update
  298.8 0.1 broadcast_compare_fusion
  298.9 1.2 copy-done
  300.0 0.4 copy.15
  300.4 139.2 %all-gather.3.cloned.1.call-done = f32[5,4096,256]{2,1,0:T(8,128)} async-done(((f32[5,256,256]{2,1,0:T(8,128)}), f32[5,4096,256]{2,1,0:T(8,128)}) %all-gather.3.cloned.1.call-update) | async-done | bytes 20971536 | tf_op jit(solution)/shard_map/all_gather | solution.py:33
  439.6 9.9 %select_bitcast_fusion = f32[5,1,256,5,1,256]{2,5,3,0,4,1:T(8,128)} fusion(f32[5,256,256]{1,2,0:T(8,128)S(1)} %copy.15, pred[5]{0:T(512)(128)(4,1)S(1)} %broadcast_compare_fusion.1, pred[5,5]{1,0:T(8,128)(4,1)S(1)} %broadcast_compare_fusion, f32[5,256,256]{2,1,0:T(8,128)S(1)} %copy-done, f32[5,16,256,256]{3,2,1,0:T(8,128)} %bitcast.63, s32[]{:T(128)S(6)} %select_n.51, ...), kind=kOutput, calls=%fused_computation.2 | convolution fusion | flops 5038080000 | bytes 17039394 | tf_op jit(solution)/shard_map/kab,cdb->kacd/dot_general | solution.py:35
  449.5 14.2 %copy.18 = f32[5,1,256,5,1,256]{5,4,3,2,1,0:T(1,128)} copy(f32[5,1,256,5,1,256]{2,5,3,0,4,1:T(8,128)} %select_bitcast_fusion) | data formatting | bytes 13107200 | tf_op jit(solution)/shard_map/broadcast_in_dim | solution.py:43
  (13 shorter events, 0.2 us)
Async XLA Ops:
  6.5 112.9 %all-reduce.4.cloned.1.call-start = ((), (), s32[]{:S(2)}) async-start(), calls=%async_computation | async-start | bytes 524288 | tf_op jit(solution)/shard_map/psum | solution.py:9
  22.4 276.3 %all-reduce.6.cloned.1.call-start = ((), (), s32[]{:S(2)}) async-start(), calls=%async_computation.1 | async-start | bytes 2621440 | tf_op jit(solution)/shard_map/psum | solution.py:9
  185.5 254.2 %all-gather.3.cloned.1.call-start = ((), (), s32[]{:S(2)}) async-start(), calls=%async_computation.2 | async-start | bytes 22282240 | tf_op jit(solution)/shard_map/all_gather | solution.py:33
  298.7 1.3 copy-start
Sparse Core Ops, SparseCore 0:
  22.5 96.8 all-reduce.3
  185.6 113.0 all-reduce.5
  301.5 138.1 all-gather.2
where the time goes:
time: 471 us; the launch traced here: 470 us
  waiting for transfers between devices  348 us (74%)
  other arithmetic  57.8 us (12%)
  local copies, waits for them, and re-layouts  37.2 us (8%)
  between operations  14.5 us (3%)
  matrix products  13 us (3%)
    psum x2, waiting for transfers between devices, broadcast(): return lax.psum(kept, axis)  208 us
    all_gather x1, waiting for transfers between devices, per_device(): every = lax.all_gather(row_tiles[:, None], 'prow', axis=1, tiled=True)  139 us
    another operation x6, other arithmetic, per_device(): factor = jnp.linalg.cholesky(leading)  34 us
    another operation x4, other arithmetic, panel_solve(): lax.linalg.triangular_solve(factor, tiles.reshape(count * width, width),...  19.8 us
    unnamed x3, local copies, waits for them, and re-layouts  15.3 us
    broadcast_in_dim x1, local copies, waits for them, and re-layouts, per_device(): return result[:, None, :, :, None, :]  14.2 us
    dot_general x1, matrix products, per_device(): jnp.einsum('kab,cdb->kacd', row_tiles, col_tiles, precision=lax.Precision...  9.87 us
  transfers between devices with their start and end apart: 3, of which 3 were waited for; matrix products, arithmetic and copies ran while one was open for 0% of the time, Pallas kernels for 0%

commit v1 on v0

--- a/solution.py
+++ b/solution.py
@@ -30,7 +30,10 @@
     factor = jnp.linalg.cholesky(leading)
     solved = panel_solve(factor, column, grid_row)
     row_tiles = broadcast(solved, "pcol", 0)
-    every = lax.all_gather(row_tiles[:, None], "prow", axis=1, tiled=True)
+    every = jnp.concatenate(
+        lax.all_to_all(jnp.stack([row_tiles[:, None]] * lax.axis_size("prow")), "prow", 0, 0),
+        axis=1,
+    )
     col_tiles = lax.dynamic_index_in_dim(every, grid_col, 1, keepdims=False)
     product = jnp.einsum("kab,cdb->kacd", row_tiles, col_tiles, precision=lax.Precision.HIGHEST)
     updated = local - product

time: 471 us -> 665 us (1.41)
  waiting for transfers between devices: 348 us -> 518 us
  local copies, waits for them, and re-layouts: 37.2 us -> 47.5 us
  starting transfers between devices: 0.09 us -> 6.75 us
    all_to_all x0 -> x1, waiting for transfers between devices: none -> 310 us  [per_device(): lax.all_to_all(jnp.stack([row_tiles[:, None]] * lax.axis_size('prow')), '...]
    all_gather x1 -> x0, waiting for transfers between devices: 139 us -> none  [per_device(): every = lax.all_gather(row_tiles[:, None], 'prow', axis=1, tiled=True)]
    another operation x6 -> x7, local copies, waits for them, and re-layouts: 4.02 us -> 14.9 us  [the longest x1 10.9 us: per_device(): jnp.stack([row_tiles[:, None]] * lax.axis_size('prow'))]
    all_to_all x0 -> x1, starting transfers between devices: none -> 6.7 us  [per_device(): lax.all_to_all(jnp.stack([row_tiles[:, None]] * lax.axis_size('prow')), '...]
    unnamed x3 -> x7, local copies, waits for them, and re-layouts: 15.3 us -> 14.8 us
where the time goes in v1:
time: 665 us; the launch traced here: 659 us
  waiting for transfers between devices  518 us (78%)
  other arithmetic  57.8 us (9%)
  local copies, waits for them, and re-layouts  47.5 us (7%)
  between operations  14.9 us (2%)
  matrix products  13 us (2%)
  starting transfers between devices  6.75 us (1%)
    all_to_all x1, waiting for transfers between devices, per_device(): lax.all_to_all(jnp.stack([row_tiles[:, None]] * lax.axis_size('prow')), '...  310 us
    psum x2, waiting for transfers between devices, broadcast(): return lax.psum(kept, axis)  208 us
    another operation x6, other arithmetic, per_device(): factor = jnp.linalg.cholesky(leading)  34 us
    another operation x4, other arithmetic, panel_solve(): lax.linalg.triangular_solve(factor, tiles.reshape(count * width, width),...  19.8 us
    unnamed x7, local copies, waits for them, and re-layouts  14.8 us
    broadcast_in_dim x1, local copies, waits for them, and re-layouts, per_device(): return result[:, None, :, :, None, :]  14.2 us
  transfers between devices with their start and end apart: 3, of which 3 were waited for; matrix products, arithmetic and copies ran while one was open for 0% of the time, Pallas kernels for 0%

profile of v1, /device:TPU:1, one launch (start us, length us, event | category | flops | bytes accessed | tf_op | source)
XLA Modules:
  0.0 658.5 jit_solution(14067524253855418750)
XLA Ops:
  6.5 0.0 all-reduce.4.cloned.1.call-start
  6.5 14.1 %copy.9 = f32[5,1,256,5,1,256]{2,5,3,0,4,1:T(8,128)} copy(f32[5,1,256,5,1,256]{5,4,3,2,1,0:T(1,128)} %param.3) | data formatting | bytes 13107200 | tf_op args[0]
  20.7 1.7 fusion.9
  22.3 0.0 all-reduce.4.cloned.1.call-update
  22.4 0.0 all-reduce.6.cloned.1.call-start
  22.4 1.4 slice.87
  23.8 0.4 copy.11
  24.3 95.1 %all-reduce.4.cloned.1.call-done = f32[256,256]{0,1:T(8,128)} async-done(((f32[256,256]{0,1:T(8,128)}), f32[256,256]{0,1:T(8,128)}) %all-reduce.4.cloned.1.call-update) | async-done | bytes 262160 | tf_op jit(solution)/shard_map/psum | solution.py:9
  119.4 1.1 copy.10
  120.5 1.0 fusion.10
  121.5 11.7 %cholesky.49 = f32[128,128]{1,0:T(8,128)S(1)} custom-call(f32[128,128]{1,0:T(8,128)S(1)} %cholesky.115), custom_call_target="Cholesky" | custom-call | tf_op jit(solution)/shard_map/jit(cholesky)/cholesky | solution.py:30
  133.2 9.8 %custom-call.14 = f32[1,128,128]{1,2,0:T(8,128)S(1)} custom-call(f32[1,128,128]{2,1,0:T(8,128)S(1)} %get-tuple-element.38), custom_call_target="InvertDiagBlocksLowerTriangular" | custom-call | tf_op jit(solution)/shard_map/jit(cholesky)/cholesky | solution.py:30
  143.1 0.2 constant_dynamic-update-slice_fusion
  143.3 0.3 convolution_subtract_fusion.1
  143.5 11.7 %cholesky.103 = f32[128,128]{1,0:T(8,128)S(1)} custom-call(f32[128,128]{1,0:T(8,128)S(1)} %convolution_subtract_fusion.1), custom_call_target="Cholesky" | custom-call | tf_op jit(solution)/shard_map/jit(cholesky)/cholesky | solution.py:30
  155.3 0.7 compare_reduce_fusion
  157.3 0.1 triangular_solve.59
  157.4 4.2 while.2
  157.5 0.7 fusion.26
  158.2 1.3 bitcast_dynamic-update-slice_fusion.2
  159.6 0.7 fusion.26
  160.2 1.3 bitcast_dynamic-update-slice_fusion.2
  161.6 19.7 %custom-call.15 = f32[2,128,128]{1,2,0:T(8,128)S(1)} custom-call(f32[2,128,128]{2,1,0:T(8,128)S(1)} %get-tuple-element.24), custom_call_target="InvertDiagBlocksLowerTriangular" | custom-call | tf_op jit(solution)/shard_map/triangular_solve | solution.py:14
  181.3 0.0 copy-start.1
  181.3 0.8 fusion.3
  182.0 0.0 copy-done.1
  182.1 1.2 convolution_subtract_fusion
  183.3 0.0 copy-start.2
  183.3 0.2 copy.12
  183.5 0.7 copy-done.2
  184.2 0.7 fusion.12
  184.8 0.1 pad_maximum_fusion
  185.0 1.2 broadcast_select_fusion
  186.1 0.0 all-reduce.6.cloned.1.call-update
  186.2 113.2 %all-reduce.6.cloned.1.call-done = f32[5,256,256]{2,1,0:T(8,128)} async-done(((f32[5,256,256]{2,1,0:T(8,128)}), f32[5,256,256]{2,1,0:T(8,128)}) %all-reduce.6.cloned.1.call-update) | async-done | bytes 1310736 | tf_op jit(solution)/shard_map/psum | solution.py:9
  299.4 10.9 %stack.3 = f32[16,5,1,256,256]{4,3,1,2,0:T(8,128)} broadcast(f32[5,256,256]{2,1,0:T(8,128)} %all-reduce.6.cloned.1.call-done), dimensions={1,3,4} | broadcast | bytes 22282240 | tf_op jit(solution)/shard_map/stack | solution.py:34
  310.3 0.0 copy-start
  310.3 6.7 %all-to-all-start = ((f32[16,5,1,256,256]{4,3,1,2,0:T(8,128)}), f32[16,5,1,256,256]{4,3,1,2,0:T(8,128)}, u32[]{:S(2)}, u32[]{:S(2)}) async-start(f32[16,5,1,256,256]{4,3,1,2,0:T(8,128)} %stack.3), calls=%async_computation | async-start | bytes 41943040 | tf_op jit(solution)/shard_map/all_to_all | solution.py:34
  317.0 0.1 broadcast_compare_fusion
  317.1 0.0 copy-done
  317.1 0.4 copy.14
  317.5 310.1 %all-to-all-done = f32[16,5,1,256,256]{4,3,1,2,0:T(8,128)} async-done(((f32[16,5,1,256,256]{4,3,1,2,0:T(8,128)}), f32[16,5,1,256,256]{4,3,1,2,0:T(8,128)}, u32[]{:S(2)}, u32[]{:S(2)}) %all-to-all-start) | async-done | bytes 20971552 | tf_op jit(solution)/shard_map/all_to_all | solution.py:34
  627.6 9.9 %select_bitcast_fusion = f32[5,1,256,5,1,256]{2,5,3,0,4,1:T(8,128)} fusion(f32[5,256,256]{1,2,0:T(8,128)S(1)} %copy.14, pred[5]{0:T(512)(128)(4,1)S(1)} %broadcast_compare_fusion.1, pred[5,5]{1,0:T(8,128)(4,1)S(1)} %broadcast_compare_fusion, f32[5,256,256]{2,1,0:T(8,128)S(1)} %copy-done, f32[16,5,1,256,256]{4,3,1,2,0:T(8,128)} %all-to-all-done, ...), kind=kOutput, calls=%fused_computation.2 | convolution fusion | flops 5038080000 | bytes 17039394 | tf_op jit(solution)/shard_map/kab,cdb->kacd/dot_general | solution.py:38
  637.5 14.2 %copy.16 = f32[5,1,256,5,1,256]{5,4,3,2,1,0:T(1,128)} copy(f32[5,1,256,5,1,256]{2,5,3,0,4,1:T(8,128)} %select_bitcast_fusion) | data formatting | bytes 13107200 | tf_op jit(solution)/shard_map/broadcast_in_dim | solution.py:46
  (13 shorter events, 0.2 us)
Async XLA Ops:
  6.5 112.9 %all-reduce.4.cloned.1.call-start = ((), (), s32[]{:S(2)}) async-start(), calls=%async_computation.1 | async-start | bytes 524288 | tf_op jit(solution)/shard_map/psum | solution.py:9
  22.4 277.0 %all-reduce.6.cloned.1.call-start = ((), (), s32[]{:S(2)}) async-start(), calls=%async_computation.2 | async-start | bytes 2621440 | tf_op jit(solution)/shard_map/psum | solution.py:9
  181.3 0.8 copy-start.1
  183.3 0.9 copy-start.2
  310.3 6.8 %copy-start = (f32[5,256,256]{2,1,0:T(8,128)S(1)}, f32[5,256,256]{2,1,0:T(8,128)}, u32[]{:S(2)}) copy-start(f32[5,256,256]{2,1,0:T(8,128)} %all-reduce.6.cloned.1.call-done) | copy-start | bytes 3932164
  310.3 317.3 %all-to-all-start = ((f32[16,5,1,256,256]{4,3,1,2,0:T(8,128)}), f32[16,5,1,256,256]{4,3,1,2,0:T(8,128)}, u32[]{:S(2)}, u32[]{:S(2)}) async-start(f32[16,5,1,256,256]{4,3,1,2,0:T(8,128)} %stack.3), calls=%async_computation | async-start | bytes 41943040 | tf_op jit(solution)/shard_map/all_to_all | solution.py:34
Sparse Core Ops, SparseCore 0:
  22.5 96.8 all-reduce.3
  186.3 113.0 all-reduce.5

commit v2 on v0

--- a/solution.py
+++ b/solution.py
@@ -6,7 +6,7 @@
 
 def broadcast(value, axis, source):
     kept = jnp.where(lax.axis_index(axis) == source, value, 0).astype(value.dtype)
-    return lax.psum(kept, axis)
+    return jnp.sum(lax.all_gather(kept, axis), axis=0)
 
 
 def panel_solve(factor, tiles, grid_row):

time: 471 us -> 427 us (0.907)
  waiting for transfers between devices: 348 us -> 310 us
  local copies, waits for them, and re-layouts: 37.2 us -> 20.4 us
  other arithmetic: 57.8 us -> 68.4 us
    psum x2 -> x0, waiting for transfers between devices: 208 us -> none  [broadcast(): return lax.psum(kept, axis)]
    all_gather x0 -> x2, waiting for transfers between devices: none -> 174 us  [broadcast(): return jnp.sum(lax.all_gather(kept, axis), axis=0)]
    reduce_sum x0 -> x2, other arithmetic: none -> 11.5 us  [broadcast(): return jnp.sum(lax.all_gather(kept, axis), axis=0)]
    unnamed x3, local copies, waits for them, and re-layouts: 15.3 us -> 6.35 us
    broadcast_in_dim x1, local copies, waits for them, and re-layouts: 14.2 us -> 8.12 us  [per_device(): return result[:, None, :, :, None, :]]
where the time goes in v2:
time: 427 us
  waiting for transfers between devices  310 us (73%)
  other arithmetic  68.4 us (16%)
  local copies, waits for them, and re-layouts  20.4 us (5%)
  between operations  14.6 us (3%)
  matrix products  12.8 us (3%)
    all_gather x2, waiting for transfers between devices, broadcast(): return jnp.sum(lax.all_gather(kept, axis), axis=0)  174 us
    all_gather x1, waiting for transfers between devices, per_device(): every = lax.all_gather(row_tiles[:, None], 'prow', axis=1, tiled=True)  136 us
    another operation x6, other arithmetic, per_device(): factor = jnp.linalg.cholesky(leading)  34 us
    another operation x4, other arithmetic, panel_solve(): lax.linalg.triangular_solve(factor, tiles.reshape(count * width, width),...  19.8 us
    reduce_sum x2, other arithmetic, broadcast(): return jnp.sum(lax.all_gather(kept, axis), axis=0)  11.5 us
    dot_general x1, matrix products, per_device(): jnp.einsum('kab,cdb->kacd', row_tiles, col_tiles, precision=lax.Precision...  9.75 us
  transfers between devices with their start and end apart: 3, of which 3 were waited for; matrix products, arithmetic and copies ran while one was open for 0% of the time, Pallas kernels for 0%

profile of v2, /device:TPU:1, one launch (start us, length us, event | category | flops | bytes accessed | tf_op | source)
XLA Modules:
  0.0 426.9 jit_solution(18267528212856591603)
XLA Ops:
  6.5 0.0 all-gather.7.cloned.1.call-start
  6.5 6.3 %copy.20 = f32[5,1,256,5,1,256]{5,2,3,0,4,1:T(8,128)} copy(f32[5,1,256,5,1,256]{5,4,3,2,1,0:T(1,128)} %param.3) | data formatting | bytes 13107200 | tf_op args[0]
  12.9 1.7 slice_select_fusion
  14.5 0.0 all-gather.7.cloned.1.call-update
  14.6 0.0 all-gather.9.cloned.1.call-start
  14.6 1.4 slice.87
  16.1 59.0 %all-gather.7.cloned.1.call-done = f32[16,256,1,256]{3,1,2,0:T(8,128)} async-done(((f32[1,256,1,256]{3,1,2,0:T(8,128)}), f32[16,256,1,256]{3,1,2,0:T(8,128)}) %all-gather.7.cloned.1.call-update) | async-done | bytes 4194320 | tf_op jit(solution)/shard_map/all_gather | solution.py:9
  75.1 2.5 reduce_sum.18
  77.5 0.1 copy.9
  77.7 11.7 %cholesky.50 = f32[128,128]{1,0:T(8,128)S(1)} custom-call(f32[128,128]{1,0:T(8,128)S(1)} %cholesky.118), custom_call_target="Cholesky" | custom-call | tf_op jit(solution)/shard_map/jit(cholesky)/cholesky | solution.py:30
  89.5 9.8 %custom-call.14 = f32[1,128,128]{1,2,0:T(8,128)S(1)} custom-call(f32[1,128,128]{2,1,0:T(8,128)S(1)} %get-tuple-element.38), custom_call_target="InvertDiagBlocksLowerTriangular" | custom-call | tf_op jit(solution)/shard_map/jit(cholesky)/cholesky | solution.py:30
  99.3 0.2 constant_dynamic-update-slice_fusion
  99.5 0.3 convolution_subtract_fusion.1
  99.8 11.7 %cholesky.105 = f32[128,128]{1,0:T(8,128)S(1)} custom-call(f32[128,128]{1,0:T(8,128)S(1)} %convolution_subtract_fusion.1), custom_call_target="Cholesky" | custom-call | tf_op jit(solution)/shard_map/jit(cholesky)/cholesky | solution.py:30
  111.6 0.7 compare_reduce_fusion
  113.7 0.1 triangular_solve.59
  113.7 4.2 while.2
  113.9 0.6 fusion.25
  114.5 1.4 bitcast_dynamic-update-slice_fusion.2
  115.9 0.6 fusion.25
  116.5 1.4 bitcast_dynamic-update-slice_fusion.2
  118.0 19.7 %custom-call.15 = f32[2,128,128]{1,2,0:T(8,128)S(1)} custom-call(f32[2,128,128]{2,1,0:T(8,128)S(1)} %get-tuple-element.24), custom_call_target="InvertDiagBlocksLowerTriangular" | custom-call | tf_op jit(solution)/shard_map/triangular_solve | solution.py:14
  137.7 0.8 fusion.3
  138.4 1.2 convolution_subtract_fusion
  139.6 0.2 copy.10
  139.9 0.7 fusion.11
  140.5 0.1 pad_maximum_fusion
  140.7 1.2 broadcast_select_fusion
  141.8 0.0 all-gather.9.cloned.1.call-update
  141.9 0.0 all-gather.11.cloned.1.call-start
  141.9 115.4 %all-gather.9.cloned.1.call-done = f32[80,256,256]{2,1,0:T(8,128)} async-done(((f32[5,256,256]{2,1,0:T(8,128)}), f32[80,256,256]{2,1,0:T(8,128)}) %all-gather.9.cloned.1.call-update) | async-done | bytes 20971536 | tf_op jit(solution)/shard_map/all_gather | solution.py:9
  257.3 9.1 %reduce_sum.19 = f32[5,256,256]{2,1,0:T(8,128)} reduce(f32[16,5,256,256]{3,2,1,0:T(8,128)} %bitcast.58, f32[]{:T(128)} %constant.116.clone.1), dimensions={0}, to_apply=%region_5.6 | reduce | flops 4915200 | bytes 22282244 | tf_op jit(solution)/shard_map/reduce_sum | solution.py:9
  266.4 0.0 copy-start
  266.4 0.0 all-gather.11.cloned.1.call-update
  266.5 0.1 broadcast_compare_fusion
  266.5 135.9 %all-gather.11.cloned.1.call-done = f32[5,4096,256]{2,1,0:T(8,128)} async-done(((f32[5,256,256]{2,1,0:T(8,128)}), f32[5,4096,256]{2,1,0:T(8,128)}) %all-gather.11.cloned.1.call-update) | async-done | bytes 20971536 | tf_op jit(solution)/shard_map/all_gather | solution.py:33
  402.5 0.0 copy-done
  402.5 9.7 %select_bitcast_fusion = f32[5,1,256,5,1,256]{5,2,3,0,4,1:T(8,128)S(1)} fusion(f32[5,256,256]{2,1,0:T(8,128)S(1)} %copy-done, pred[5]{0:T(512)(128)(4,1)S(1)} %broadcast_compare_fusion.1, pred[5,5]{1,0:T(8,128)(4,1)S(1)} %broadcast_compare_fusion, f32[5,16,256,256]{3,2,1,0:T(8,128)} %bitcast.66, s32[]{:T(128)S(6)} %select_n.58, ...), kind=kOutput, calls=%fused_computation.3 | convolution fusion | flops 5038080000 | bytes 17040900 | tf_op jit(solution)/shard_map/kab,cdb->kacd/dot_general | solution.py:35
  412.2 8.1 %copy.13 = f32[5,1,256,5,1,256]{5,4,3,2,1,0:T(1,128)} copy(f32[5,1,256,5,1,256]{5,2,3,0,4,1:T(8,128)S(1)} %select_bitcast_fusion) | data formatting | bytes 13107200 | tf_op jit(solution)/shard_map/broadcast_in_dim | solution.py:43
  (14 shorter events, 0.2 us)
Async XLA Ops:
  6.5 68.5 %all-gather.7.cloned.1.call-start = ((), (), s32[]{:S(2)}) async-start(), calls=%async_computation | async-start | bytes 4456448 | tf_op jit(solution)/shard_map/all_gather | solution.py:9
  14.6 242.8 %all-gather.9.cloned.1.call-start = ((), (), s32[]{:S(2)}) async-start(), calls=%async_computation.1 | async-start | bytes 22282240 | tf_op jit(solution)/shard_map/all_gather | solution.py:9
  141.9 260.6 %all-gather.11.cloned.1.call-start = ((), (), s32[]{:S(2)}) async-start(), calls=%async_computation.2 | async-start | bytes 22282240 | tf_op jit(solution)/shard_map/all_gather | solution.py:33
  266.4 136.1 %copy-start = (f32[5,256,256]{2,1,0:T(8,128)S(1)}, f32[5,256,256]{2,1,0:T(8,128)}, u32[]{:S(2)}) copy-start(f32[5,256,256]{2,1,0:T(8,128)} %reduce_sum.19) | copy-start | bytes 3932164
Sparse Core Ops, SparseCore 0:
  14.7 60.3 all-gather.6
  142.0 115.3 all-gather.8
  266.6 135.8 all-gather.10
